TPU v7x, 32 devices: a whole 2x2x4 slice. The times are simulated.
32 devices in a mesh: groups: 2 (over x), dom: 16 (over z, y, core).
Axes of the slice: x: 2, y: 2, z: 4, core: 2. Of those that a mesh axis runs over, the one named last changes fastest.
Arguments:
- features: bfloat16 [16384, 2048], P(('groups', 'dom')), parts along dimension 0, may hold values from -6 to 6
- cotangent: bfloat16 [16384, 2048], P(('groups', 'dom')), parts along dimension 0, may hold values from -0.5 to 0.5
- positions: bfloat16 [3, 16384], P(None, ('groups', 'dom')), parts along dimension 1, may hold values from 0 to 1
- value_weight: bfloat16 [4, 128, 128], replicated, may hold values from -0.5 to 0.5
- query_weight: bfloat16 [128, 128], replicated, may hold values from -0.5 to 0.5
- key_weight: bfloat16 [128, 128], replicated, may hold values from -0.5 to 0.5
- ghost_index: int32 [32, 2, 256], P(('groups', 'dom')), parts along dimension 0, may hold values from 0 to 511, as said below
- tile_pairs: int32 [32, 3, 8, 2], P(('groups', 'dom')), parts along dimension 0, may hold values from 0 to 3, as said below
- tile_counts: int32 [32, 3], P(('groups', 'dom')), parts along dimension 0, may hold values from 1 to 8, as said below
Outputs:
- feat_adjoint: bfloat16 [16384, 2048], P(('groups', 'dom')), parts along dimension 0
- forces: float32 [3, 16384], P(None, ('groups', 'dom')), parts along dimension 1
There are 2 independent parts, one for each index of `groups`. A program takes and returns all parts, laid end to end along the dimension named above; an argument that names none is the same for every part. Nothing has to cross between parts.
Inputs may be any that keep to these rules, and one draw needn't show every extreme that they name: Each list ghost_index[d, k, :] names 256 different local atoms of domain d. tile_pairs[d, 0, :] holds different pairs (a, b) with a <= b; for k >= 1, tile_pairs[d, k, :] holds all pairs with a < 4 and b < 2, each once. Only the first tile_counts[d, k] slots of tile_pairs[d, k] are used; in every round some domain uses all 8.
All inputs are finite; a program needn't handle non-finite values.
Results may differ from a plain program's by a relative error of at most 0.0064.
Values may be sent and summed in bfloat16 or wider, within the bound.
A program may use at most 128 MiB of HBM per device.

v0:
```python
import functools

import jax
import jax.numpy as jnp
from jax import lax
from jax.experimental import pallas as pl
from jax.experimental.pallas import tpu as pltpu
from jax.sharding import PartitionSpec as P

TILE = 128
CUTOFF_SQ = 9.0
CHUNKS = 2
VMEM_BYTES = 48 * 2**20
F32 = jnp.float32
BF16 = jnp.bfloat16


def dot_nt(left, right):
    return lax.dot_general(left, right, (((1,), (1,)), ((), ())), preferred_element_type=F32)


def dot_tn(left, right):
    return lax.dot_general(left, right, (((0,), (0,)), ((), ())), preferred_element_type=F32)


def dot_nn(left, right):
    return lax.dot_general(left, right, (((1,), (0,)), ((), ())), preferred_element_type=F32)


def project_kernel(feat_ref, vw_ref, qw_ref, kw_ref, val_ref, qry_ref, key_ref):
    chan = vw_ref.shape[1]
    for comp in range(16):
        cols = slice(comp * chan, (comp + 1) * chan)
        degree = int(comp**0.5)
        val_ref[:, cols] = dot_nn(feat_ref[:, cols], vw_ref[degree]).astype(BF16)
    scalars = feat_ref[:, :chan]
    qry_ref[...] = dot_nn(scalars, qw_ref[...]).astype(BF16)
    key_ref[...] = dot_nn(scalars, kw_ref[...]).astype(BF16)


def final_kernel(u_ref, q_ref, k_ref, vw_ref, qw_ref, kw_ref, out_ref):
    chan = vw_ref.shape[1]
    for comp in range(16):
        cols = slice(comp * chan, (comp + 1) * chan)
        degree = int(comp**0.5)
        mixed = dot_nt(u_ref[:, cols].astype(BF16), vw_ref[degree])
        if comp == 0:
            mixed += dot_nt(q_ref[...].astype(BF16), qw_ref[...])
            mixed += dot_nt(k_ref[...].astype(BF16), kw_ref[...])
        out_ref[:, cols] = mixed.astype(BF16)


def block_kernel(chunks, own, first, scale, *refs):
    val_ref, key_ref, pt_ref, row_ref = refs[:4]
    refs = refs[4:]
    cot_refs, refs = refs[:chunks], refs[chunks:]
    qry_ref, ps_ref, col_ref = refs[:3]
    refs = refs[3:]
    if not first:
        u_in, k_in, p_in = refs[:3]
        refs = refs[3:]
    u_out, k_out, p_out, q_src, p_src = refs
    atoms = val_ref.shape[0]
    step = TILE * 2
    rows_chunk = atoms // chunks
    q_src[...] = jnp.zeros_like(q_src)
    p_src[...] = jnp.zeros_like(p_src)
    nmask = row_ref.shape[1]
    for c in range(chunks):
        src = slice(c * rows_chunk, (c + 1) * rows_chunk)
        cot = cot_refs[c]
        for r in range(atoms // step):
            tgt = slice(r * step, (r + 1) * step)
            grad = dot_nt(val_ref[tgt, :], cot[...])
            score = scale * dot_nt(key_ref[tgt, :], qry_ref[src, :])
            diffs = [pt_ref[tgt, x : x + 1] - ps_ref[x : x + 1, src] for x in range(3)]
            dist = diffs[0] * diffs[0] + diffs[1] * diffs[1] + diffs[2] * diffs[2]
            inside = jnp.maximum(1.0 - dist * (1.0 / CUTOFF_SQ), 0.0)
            keep = row_ref[tgt, 0:1] * col_ref[0:1, src]
            for b in range(1, nmask):
                keep += row_ref[tgt, b : b + 1] * col_ref[b : b + 1, src]
            if own:
                row_id = lax.broadcasted_iota(jnp.int32, keep.shape, 0) + r * step
                col_id = lax.broadcasted_iota(jnp.int32, keep.shape, 1) + c * rows_chunk
                keep = jnp.where(row_id == col_id, 0.0, keep)
            gate = jax.nn.sigmoid(score)
            kept = keep * inside
            half = kept * gate
            weight = half * inside
            zgrad = (grad * weight * (1.0 - gate)).astype(BF16)
            push = (-4.0 / CUTOFF_SQ) * grad * half
            weight = weight.astype(BF16)
            upd = dot_nn(weight, cot[...])
            kup = scale * dot_nn(zgrad, qry_ref[src, :])
            fresh = first and c == 0
            base_u, base_k, base_p = (u_out, k_out, p_out) if c else (None,) * 3
            if c == 0 and not first:
                base_u, base_k, base_p = u_in, k_in, p_in
            if fresh:
                u_out[tgt, :] = upd
                k_out[tgt, :] = kup
            else:
                u_out[tgt, :] = base_u[tgt, :] + upd
                k_out[tgt, :] = base_k[tgt, :] + kup
            q_src[src, :] += scale * dot_tn(zgrad, key_ref[tgt, :])
            for x in range(3):
                term = push * diffs[x]
                across = jnp.sum(term, axis=1, keepdims=True)
                if fresh:
                    p_out[tgt, x : x + 1] = across
                else:
                    p_out[tgt, x : x + 1] = base_p[tgt, x : x + 1] + across
                p_src[x : x + 1, src] -= jnp.sum(term, axis=0, keepdims=True)


def whole(n):
    return [pl.BlockSpec(memory_space=pltpu.VMEM)] * n


def run_block(own_side, row_mask, cots, block_small, sums, own, scale):
    values, keys, pt = own_side
    qry, ps, col_mask = block_small
    atoms, feat = values.shape
    width = keys.shape[1]
    first = sums is None
    args = [values, keys, pt, row_mask, *cots, qry, ps, col_mask]
    if not first:
        args += list(sums)
    out = [
        jax.ShapeDtypeStruct((atoms, feat), F32),
        jax.ShapeDtypeStruct((atoms, width), F32),
        jax.ShapeDtypeStruct((atoms, 8), F32),
        jax.ShapeDtypeStruct((atoms, width), F32),
        jax.ShapeDtypeStruct((8, atoms), F32),
    ]
    u, k, p, qs, psrc = pl.pallas_call(
        functools.partial(block_kernel, len(cots), own, first, scale),
        out_shape=out,
        in_specs=whole(len(args)),
        out_specs=whole(5),
        compiler_params=pltpu.CompilerParams(vmem_limit_bytes=VMEM_BYTES),
        cost_estimate=pl.CostEstimate(
            flops=4 * atoms * atoms * feat, bytes_accessed=14 * 2**20, transcendentals=atoms * atoms
        ),
    )(*args)
    return (u, k, p), (qs, psrc)


def shards(
    features, cotangent, positions, value_weight, query_weight, key_weight, ghost_index, tile_pairs, tile_counts
):
    atoms, feat = features.shape
    chan = value_weight.shape[1]
    width = query_weight.shape[1]
    scale = width ** (-0.5)
    slots = tile_pairs.shape[2]
    tiles = atoms // TILE
    gtiles = ghost_index.shape[2] // TILE
    domains = lax.axis_size("dom")
    me = lax.axis_index("dom")
    core = me % 2
    side = (me // 2) % 2

    def bit(i, b):
        return (i >> b) & 1

    def send(block, rule):
        return lax.ppermute(block, "dom", [(i, rule(i) % domains) for i in range(domains)])

    across = lambda i: i ^ 2
    along = lambda i: i + 4 if bit(i, 1) == 0 else i - 4
    twin = lambda i: i ^ 1
    back_far = lambda i: i - 2 if bit(i, 1) == 0 else i + 2
    back_near = lambda i: i - 1 if bit(i, 0) == 0 else i + 1

    values, queries, keys = pl.pallas_call(
        project_kernel,
        out_shape=[
            jax.ShapeDtypeStruct((atoms, feat), BF16),
            jax.ShapeDtypeStruct((atoms, width), BF16),
            jax.ShapeDtypeStruct((atoms, width), BF16),
        ],
        in_specs=whole(4),
        out_specs=whole(3),
        compiler_params=pltpu.CompilerParams(vmem_limit_bytes=VMEM_BYTES),
    )(features, value_weight, query_weight, key_weight)

    used = jnp.arange(slots, dtype=jnp.int32)[None, :] < tile_counts[0][:, None]
    ids = jnp.arange(tiles, dtype=jnp.int32)
    hit_a = tile_pairs[0, :, :, 0, None] == ids
    hit_b = tile_pairs[0, :, :, 1, None] == ids
    active = jnp.sum(
        (hit_a[:, :, :, None] & hit_b[:, :, None, :] & used[:, :, None, None]).astype(F32), axis=1
    )
    intra = jnp.maximum(active[0], active[0].T)
    atom_ids = jnp.arange(atoms, dtype=jnp.int32)
    listed = ghost_index[0].reshape(2, gtiles, TILE)
    ghost_rows = jnp.sum((listed[:, :, :, None] == atom_ids).astype(F32), axis=2)
    act_rows = jnp.repeat(active[1:, :, :gtiles].transpose(0, 2, 1), TILE, axis=2)

    small = jnp.concatenate(
        [
            queries,
            positions.reshape(3 * atoms // 128, 128),
            jnp.zeros((4, 128), BF16),
            ghost_rows.astype(BF16).reshape(-1, 128),
            act_rows.astype(BF16).reshape(-1, 128),
        ],
        axis=0,
    )
    small_1 = send(small, across)
    small_0 = send(small, twin)
    small_3 = send(small_1, along)
    straight = (side == 0) == (core == 0)
    small_p = send(jnp.where(straight, small_1, small_3), twin)

    rows = atoms // CHUNKS
    cut = lambda c: cotangent[c * rows : (c + 1) * rows]
    cot_0 = send(cotangent, twin)
    cot_1, cot_3, cot_p = [], [], []
    for c in range(CHUNKS):
        cot_1.append(send(cut(c), across))
        cot_3.append(send(cot_1[c], along))
        cot_p.append(send(jnp.where(straight, cot_1[c], cot_3[c]), twin))

    points = positions.astype(F32)
    pt = jnp.pad(points.T, ((0, 0), (0, 5)))
    own_side = (values, keys, pt)

    def unpack(pack, step, forward):
        qry = pack[:atoms]
        pos = pack[atoms : atoms + 3 * atoms // 128].reshape(3, atoms).astype(F32)
        shift = jnp.where(forward, step, -step).astype(F32)
        ps = jnp.pad(pos + jnp.array([1.0, 0.0, 0.0], F32)[:, None] * shift, ((0, 5), (0, 0)))
        marks = pack[atoms + 3 * atoms // 128 + 4 :].astype(F32).reshape(2, 2, gtiles, atoms)[:, step - 1]
        col = jnp.where(forward, marks[0], marks[1])
        row = jnp.where(forward, act_rows[step - 1], ghost_rows[step - 1])
        return (qry, ps, jnp.pad(col, ((0, 8 - gtiles), (0, 0)))), row.T

    one_hot = jnp.repeat(jnp.eye(tiles, dtype=F32), TILE, axis=1)
    own_small = (queries, jnp.pad(points, ((0, 5), (0, 0))), jnp.pad(one_hot, ((0, 8 - tiles), (0, 0))))
    own_rows = jnp.repeat(intra, TILE, axis=0)

    def pack_back(src):
        qs, ps = src
        return jnp.concatenate([qs, ps[:4].reshape(-1, 128)], axis=0).astype(BF16)

    sums, own_src = run_block(own_side, own_rows, [cotangent], own_small, None, True, scale)
    plan = [
        (small_0, [cot_0], 1, core == 0, twin),
        (small_1, cot_1, 2, side == 0, across),
        (small_3, cot_3, 2, side == 1, back_far),
        (small_p, cot_p, 1, core == 1, back_near),
    ]
    returned = []
    for pack, cots, step, forward, back in plan:
        block_small, row = unpack(pack, step, forward)
        sums, src = run_block(own_side, row, cots, block_small, sums, False, scale)
        returned.append(send(pack_back(src), back))
    sum_u, sum_k, sum_p = sums
    sum_q, p_src = own_src
    sum_p = sum_p[:, :3].T + p_src[:3]
    for pack in returned:
        sum_q = sum_q + pack[:atoms].astype(F32)
        sum_p = sum_p + pack[atoms:].astype(F32).reshape(4, atoms)[:3]
    adjoint = pl.pallas_call(
        final_kernel,
        out_shape=jax.ShapeDtypeStruct((atoms, feat), BF16),
        in_specs=whole(6),
        out_specs=pl.BlockSpec(memory_space=pltpu.VMEM),
        compiler_params=pltpu.CompilerParams(vmem_limit_bytes=VMEM_BYTES),
    )(sum_u, sum_q, sum_k, value_weight, query_weight, key_weight)
    return adjoint, -sum_p


def solution(mesh):
    both = ("groups", "dom")
    placed = (
        P(both, None),
        P(both, None),
        P(None, both),
        P(),
        P(),
        P(),
        P(both, None, None),
        P(both, None, None, None),
        P(both, None),
    )
    return jax.shard_map(
        shards, mesh=mesh, in_specs=placed, out_specs=(P(both, None), P(None, both)), check_vma=False
    )
```

profile of v0, /device:TPU:0, one launch (start us, length us, event | category | flops | bytes accessed | tf_op | source)
XLA Modules:
  0.0 189.0 jit_solution(15782483706763353975)
XLA Ops:
  4.1 1.6 copy-done.2
  9.0 3.8 %concatenate.19 = bf16[560,128]{1,0:T(8,128)(2,1)} concatenate(bf16[512,128]{1,0:T(8,128)(2,1)S(1)} %get-tuple-element.32.refs_5_, bf16[12,128]{1,0:T(8,128)(2,1)S(1)} %reshape.158, bf16[4,128]{1,0:T(4,128)(2,1)S(1)} %broadcast_in_dim.33, bf16[16,128]{1,0:T(8,128)(2,1)S(1)} %convert_element_type.106, bf16[16,128]{1,0:T(8,128)(2,1)S(1)} %broadcast_in_dim.34), dimensions={0} | concatenate | bytes 286720 | tf_op jit(solution)/shard_map/concatenate | solution.py:201
  13.2 2.5 %collective-permute-start.6 = (bf16[560,128]{1,0:T(8,128)(2,1)}, bf16[560,128]{1,0:T(8,128)(2,1)}, u32[]{:S(2)}, u32[]{:S(2)}) collective-permute-start(bf16[560,128]{1,0:T(8,128)(2,1)} %concatenate.19), channel_id=1, source_target_pairs={{0,2},{1,3},{2,0},{3,1},{4,6},{5,7},{6,4},{7,5},{8,10},{9,11},{10,... | collective-permute-start | bytes 430088 | tf_op jit(solution)/shard_map/ppermute | solution.py:168
  16.0 3.1 %fusion.10 = (bf16[256,2048]{1,0:T(8,128)(2,1)}, bf16[256,2048]{1,0:T(8,128)(2,1)}) fusion(bf16[512,2048]{1,0:T(8,128)(2,1)} %refs_4_.1), kind=kLoop, calls=%fused_computation.68 | loop fusion | bytes 4194304 | tf_op jit(solution)/shard_map/slice | solution.py:218
  19.4 1.7 collective-permute-start.3
  29.7 1.3 copy.65
  31.1 1.5 copy.79
  33.3 1.6 copy-done.3
  36.5 5.4 %shard_map.141 = (f32[512,2048]{1,0:T(8,128)}, f32[512,128]{1,0:T(8,128)S(1)}, f32[512,8]{1,0:T(8,128)S(1)}, f32[512,128]{1,0:T(8,128)S(1)}, f32[8,512]{1,0:T(8,128)S(1)}) custom-call(bf16[512,2048]{1,0:T(8,128)(2,1)S(1)} %get-tuple-element.30.refs_0_, bf16[512,128]{1,0:T(8,128)(2,1)S(1)} %get-tuple-element.31.refs_1_, f32[512,8]{1,0:T(8,128)S(1)} %pad.37.refs_2_, ...), custom_call_target="tpu_custom_call" | custom-call | flops 2147483648 | bytes 14680064 | tf_op jit(solution)/shard_map/pallas_call | solution.py:136
  44.8 1.8 bitcast_select_fusion.2
  46.6 1.8 bitcast_select_fusion
  57.7 1.6 collective-permute-start.7
  63.0 1.6 slice.279.refs_5_
  64.6 1.6 slice.274.refs_6_
  71.8 1.6 slice.269.refs_6_
  73.4 1.6 collective-permute-start.4
  76.4 1.3 slice_convert_fusion.7
  77.7 1.3 reshape.175
  79.0 1.6 collective-permute-start.1
  81.9 1.6 slice.262.refs_6_
  88.7 8.1 %shard_map.142 = (f32[512,2048]{1,0:T(8,128)}, f32[512,128]{1,0:T(8,128)S(1)}, f32[512,8]{1,0:T(8,128)S(1)}, f32[512,128]{1,0:T(8,128)S(1)}, f32[8,512]{1,0:T(8,128)S(1)}) custom-call(bf16[512,2048]{1,0:T(8,128)(2,1)S(1)} %get-tuple-element.30.refs_0_, bf16[512,128]{1,0:T(8,128)(2,1)S(1)} %get-tuple-element.31.refs_1_, f32[512,8]{1,0:T(8,128)S(1)} %pad.37.refs_2_, ...), custom_call_target="tpu_custom_call" | custom-call | flops 2147483648 | bytes 14680064 | tf_op jit(solution)/shard_map/pallas_call | solution.py:136
  98.9 2.6 %collective-permute-done.4.refs_5_ = bf16[256,2048]{1,0:T(8,128)(2,1)} collective-permute-done((bf16[256,2048]{1,0:T(8,128)(2,1)}, bf16[256,2048]{1,0:T(8,128)(2,1)}, u32[]{:S(2)}, u32[]{:S(2)}) %collective-permute-start.4) | collective-permute-done | bytes 1048608 | tf_op jit(solution)/shard_map/ppermute | solution.py:168
  101.5 2.3 %broadcast_select_fusion = bf16[256,2048]{1,0:T(8,128)(2,1)} fusion(bf16[256,2048]{1,0:T(8,128)(2,1)} %collective-permute-done.3.refs_5_, bf16[256,2048]{1,0:T(8,128)(2,1)} %collective-permute-done.4.refs_5_, pred[]{:T(512)S(6)} %eq.91), kind=kLoop, calls=%fused_computation.2 | loop fusion | flops 524288 | bytes 3145729 | tf_op jit(solution)/shard_map/jit(_where)/select_n | solution.py:224
  103.9 19.7 %collective-permute-done.1.refs_4_ = bf16[256,2048]{1,0:T(8,128)(2,1)} collective-permute-done((bf16[256,2048]{1,0:T(8,128)(2,1)S(1)}, bf16[256,2048]{1,0:T(8,128)(2,1)}, u32[]{:S(2)}, u32[]{:S(2)}) %collective-permute-start.1) | collective-permute-done | bytes 1048608 | tf_op jit(solution)/shard_map/ppermute | solution.py:168
  125.7 9.5 %shard_map.143 = (f32[512,2048]{1,0:T(8,128)}, f32[512,128]{1,0:T(8,128)S(1)}, f32[512,8]{1,0:T(8,128)S(1)}, f32[512,128]{1,0:T(8,128)S(1)}, f32[8,512]{1,0:T(8,128)S(1)}) custom-call(bf16[512,2048]{1,0:T(8,128)(2,1)} %copy-done, bf16[512,128]{1,0:T(8,128)(2,1)S(1)} %get-tuple-element.31.refs_1_, f32[512,8]{1,0:T(8,128)S(1)} %pad.37.refs_2_, ...), custom_call_target="tpu_custom_call" | custom-call | flops 2147483648 | bytes 14680064 | tf_op jit(solution)/shard_map/pallas_call | solution.py:136
  142.9 9.9 %shard_map.144 = (f32[512,2048]{1,0:T(8,128)}, f32[512,128]{1,0:T(8,128)S(1)}, f32[512,8]{1,0:T(8,128)S(1)}, f32[512,128]{1,0:T(8,128)S(1)}, f32[8,512]{1,0:T(8,128)S(1)}) custom-call(bf16[512,2048]{1,0:T(8,128)(2,1)} %copy-done, bf16[512,128]{1,0:T(8,128)(2,1)S(1)} %get-tuple-element.31.refs_1_, f32[512,8]{1,0:T(8,128)S(1)} %pad.37.refs_2_, ...), custom_call_target="tpu_custom_call" | custom-call | flops 2147483648 | bytes 14680064 | tf_op jit(solution)/shard_map/pallas_call | solution.py:136
  154.2 1.7 collective-permute-start.13
  163.6 9.8 %shard_map.145 = (f32[512,2048]{1,0:T(8,128)}, f32[512,128]{1,0:T(8,128)S(1)}, f32[512,8]{1,0:T(8,128)S(1)}, f32[512,128]{1,0:T(8,128)S(1)}, f32[8,512]{1,0:T(8,128)S(1)}) custom-call(bf16[512,2048]{1,0:T(8,128)(2,1)} %copy-done, bf16[512,128]{1,0:T(8,128)(2,1)S(1)} %get-tuple-element.31.refs_1_, f32[512,8]{1,0:T(8,128)S(1)} %pad.37.refs_2_, ...), custom_call_target="tpu_custom_call" | custom-call | flops 2147483648 | bytes 14680064 | tf_op jit(solution)/shard_map/pallas_call | solution.py:136
  174.2 2.6 %collective-permute-start.14 = (bf16[528,128]{1,0:T(8,128)(2,1)S(1)}, bf16[528,128]{1,0:T(8,128)(2,1)S(1)}, u32[]{:S(2)}, u32[]{:S(2)}) collective-permute-start(bf16[528,128]{1,0:T(8,128)(2,1)S(1)} %pad_maximum_fusion.3), channel_id=1, source_target_pairs={{0,15},{1,2},{2,1},{3,4},{4,3},{5,6},{6,5},{7,8},{8,7},{9,10},{10,... | collective-permute-start | bytes 405512 | tf_op jit(solution)/shard_map/ppermute | solution.py:168
  177.6 3.8 %collective-permute-done.14 = bf16[528,128]{1,0:T(8,128)(2,1)S(1)} collective-permute-done((bf16[528,128]{1,0:T(8,128)(2,1)S(1)}, bf16[528,128]{1,0:T(8,128)(2,1)S(1)}, u32[]{:S(2)}, u32[]{:S(2)}) %collective-permute-start.14) | collective-permute-done | bytes 135200 | tf_op jit(solution)/shard_map/ppermute | solution.py:168
  184.7 2.2 %copy-done.1 = f32[512,2048]{1,0:T(8,128)S(1)} copy-done((f32[512,2048]{1,0:T(8,128)S(1)}, f32[512,2048]{1,0:T(8,128)}, u32[]{:S(2)}) %copy-start.1) | copy-done | bytes 4194328
  186.9 2.1 %shard_map.146 = bf16[512,2048]{1,0:T(8,128)(2,1)} custom-call(f32[512,2048]{1,0:T(8,128)S(1)} %copy-done.1, f32[512,128]{1,0:T(8,128)S(1)} %convert_add_fusion.q_ref, f32[512,128]{1,0:T(8,128)S(1)} %get-tuple-element.55.k_ref, bf16[4,128,128]{2,1,0:T(8,128)(2,1)S(1)} %copy-done.13, bf16[128,128]{1,0:T(8,128)(2,1)S(1)} %copy-done.34, ...), custom_call_target="tpu_custom_call" | custom-call | tf_op jit(solution)/shard_map/pallas_call | solution.py:266
  (218 shorter events, 74.0 us)
Async XLA Ops:
  8.9 10.2 %copy-start.37 = (bf16[512,128]{1,0:T(8,128)(2,1)}, bf16[512,128]{1,0:T(8,128)(2,1)S(1)}, u32[]{:S(2)}) copy-start(bf16[512,128]{1,0:T(8,128)(2,1)S(1)} %get-tuple-element.32.refs_5_) | copy-start | bytes 393220
  8.9 74.6 %copy-start = (bf16[512,2048]{1,0:T(8,128)(2,1)}, bf16[512,2048]{1,0:T(8,128)(2,1)S(1)}, u32[]{:S(2)}) copy-start(bf16[512,2048]{1,0:T(8,128)(2,1)S(1)} %get-tuple-element.30.refs_0_) | copy-start | bytes 6291460
  12.8 8.9 %copy-start.49 = (bf16[3,512]{1,0:T(4,128)(2,1)S(1)}, bf16[3,512]{1,0:T(4,128)(2,1)}, u32[]{:S(2)}) copy-start(bf16[3,512]{1,0:T(4,128)(2,1)} %param.15) | copy-start | bytes 9220
  12.8 36.9 %collective-permute-start.10 = (bf16[560,128]{1,0:T(8,128)(2,1)}, bf16[560,128]{1,0:T(8,128)(2,1)}, u32[]{:S(2)}, u32[]{:S(2)}) collective-permute-start(bf16[560,128]{1,0:T(8,128)(2,1)} %concatenate.19), channel_id=1, source_target_pairs={{0,1},{1,0},{2,3},{3,2},{4,5},{5,4},{6,7},{7,6},{8,9},{9,8},{10,11... | collective-permute-start | bytes 430088 | tf_op jit(solution)/shard_map/ppermute | solution.py:168
  13.2 40.3 %collective-permute-start.6 = (bf16[560,128]{1,0:T(8,128)(2,1)}, bf16[560,128]{1,0:T(8,128)(2,1)}, u32[]{:S(2)}, u32[]{:S(2)}) collective-permute-start(bf16[560,128]{1,0:T(8,128)(2,1)} %concatenate.19), channel_id=1, source_target_pairs={{0,2},{1,3},{2,0},{3,1},{4,6},{5,7},{6,4},{7,5},{8,10},{9,11},{10,... | collective-permute-start | bytes 430088 | tf_op jit(solution)/shard_map/ppermute | solution.py:168
  15.8 67.7 %collective-permute-start.9 = (bf16[512,2048]{1,0:T(8,128)(2,1)}, bf16[512,2048]{1,0:T(8,128)(2,1)}, u32[]{:S(2)}, u32[]{:S(2)}) collective-permute-start(bf16[512,2048]{1,0:T(8,128)(2,1)} %refs_4_.1), channel_id=1, source_target_pairs={{0,1},{1,0},{2,3},{3,2},{4,5},{5,4},{6,7},{7,6},{8,9},{9,8},{10,11... | collective-permute-start | bytes 6291464 | tf_op jit(solution)/shard_map/ppermute | solution.py:168
  19.1 59.9 %collective-permute-start = (bf16[256,2048]{1,0:T(8,128)(2,1)}, bf16[256,2048]{1,0:T(8,128)(2,1)S(1)}, u32[]{:S(2)}, u32[]{:S(2)}) collective-permute-start(bf16[256,2048]{1,0:T(8,128)(2,1)} %get-tuple-element.67), channel_id=1, source_target_pairs={{0,2},{1,3},{2,0},{3,1},{4,6},{5,7},{6,4},{7,5},{8,10},{9,11},{10,... | collective-permute-start | bytes 3145736 | tf_op jit(solution)/shard_map/ppermute | solution.py:168
  19.4 54.0 %collective-permute-start.3 = (bf16[256,2048]{1,0:T(8,128)(2,1)}, bf16[256,2048]{1,0:T(8,128)(2,1)}, u32[]{:S(2)}, u32[]{:S(2)}) collective-permute-start(bf16[256,2048]{1,0:T(8,128)(2,1)} %get-tuple-element.66), channel_id=1, source_target_pairs={{0,2},{1,3},{2,0},{3,1},{4,6},{5,7},{6,4},{7,5},{8,10},{9,11},{10,... | collective-permute-start | bytes 3145736 | tf_op jit(solution)/shard_map/ppermute | solution.py:168
  33.3 1.6 copy-start.3
  57.7 8.5 %collective-permute-start.7 = (bf16[560,128]{1,0:T(8,128)(2,1)}, bf16[560,128]{1,0:T(8,128)(2,1)S(1)}, u32[]{:S(2)}, u32[]{:S(2)}) collective-permute-start(bf16[560,128]{1,0:T(8,128)(2,1)} %collective-permute-done.6), channel_id=1, source_target_pairs={{0,4},{1,5},{2,14},{3,15},{4,8},{5,9},{6,2},{7,3},{8,12},{9,13},{1... | collective-permute-start | bytes 430088 | tf_op jit(solution)/shard_map/ppermute | solution.py:168
  70.4 4.5 %collective-permute-start.8 = (bf16[560,128]{1,0:T(8,128)(2,1)S(1)}, bf16[560,128]{1,0:T(8,128)(2,1)S(1)}, u32[]{:S(2)}, u32[]{:S(2)}) collective-permute-start(bf16[560,128]{1,0:T(8,128)(2,1)S(1)} %broadcast_select_fusion.2), channel_id=1, source_target_pairs={{0,1},{1,0},{2,3},{3,2},{4,5},{5,4},{6,7},{7,6},{8,9},{9,8},{10,11... | collective-permute-start | bytes 430088 | tf_op jit(solution)/shard_map/ppermute | solution.py:168
  73.4 28.1 %collective-permute-start.4 = (bf16[256,2048]{1,0:T(8,128)(2,1)}, bf16[256,2048]{1,0:T(8,128)(2,1)}, u32[]{:S(2)}, u32[]{:S(2)}) collective-permute-start(bf16[256,2048]{1,0:T(8,128)(2,1)} %collective-permute-done.3.refs_5_), channel_id=1, source_target_pairs={{0,4},{1,5},{2,14},{3,15},{4,8},{5,9},{6,2},{7,3},{8,12},{9,13},{1... | collective-permute-start | bytes 3145736 | tf_op jit(solution)/shard_map/ppermute | solution.py:168
  79.0 44.5 %collective-permute-start.1 = (bf16[256,2048]{1,0:T(8,128)(2,1)S(1)}, bf16[256,2048]{1,0:T(8,128)(2,1)}, u32[]{:S(2)}, u32[]{:S(2)}) collective-permute-start(bf16[256,2048]{1,0:T(8,128)(2,1)S(1)} %collective-permute-done.refs_4_), channel_id=1, source_target_pairs={{0,4},{1,5},{2,14},{3,15},{4,8},{5,9},{6,2},{7,3},{8,12},{9,13},{1... | collective-permute-start | bytes 3145736 | tf_op jit(solution)/shard_map/ppermute | solution.py:168
  98.9 57.1 %collective-permute-start.11 = (bf16[528,128]{1,0:T(8,128)(2,1)}, bf16[528,128]{1,0:T(8,128)(2,1)}, u32[]{:S(2)}, u32[]{:S(2)}) collective-permute-start(bf16[528,128]{1,0:T(8,128)(2,1)} %pad_maximum_fusion), channel_id=1, source_target_pairs={{0,1},{1,0},{2,3},{3,2},{4,5},{5,4},{6,7},{7,6},{8,9},{9,8},{10,11... | collective-permute-start | bytes 405512 | tf_op jit(solution)/shard_map/ppermute | solution.py:168
  103.8 21.9 %copy-start.6 = (f32[2,512]{0,1:T(8,128)S(1)}, f32[2,512]{0,1:T(8,128)}, u32[]{:S(2)}) copy-start(f32[2,512]{0,1:T(8,128)} %get-tuple-element.70) | copy-start | bytes 12292
  103.8 21.9 %copy-start.10 = (bf16[512,128]{1,0:T(8,128)(2,1)S(1)}, bf16[512,128]{1,0:T(8,128)(2,1)}, u32[]{:S(2)}) copy-start(bf16[512,128]{1,0:T(8,128)(2,1)} %slice.274.refs_6_) | copy-start | bytes 393220
  103.8 21.9 %copy-start.23 = (f32[512,128]{1,0:T(8,128)S(1)}, f32[512,128]{1,0:T(8,128)}, u32[]{:S(2)}) copy-start(f32[512,128]{1,0:T(8,128)} %copy-done.22) | copy-start | bytes 786436
  103.8 21.9 %copy-start.25 = (f32[512,8]{1,0:T(8,128)S(1)}, f32[512,8]{1,0:T(8,128)}, u32[]{:S(2)}) copy-start(f32[512,8]{1,0:T(8,128)} %copy-done.24) | copy-start | bytes 49156
  103.8 21.9 %copy-start.41 = (f32[8,512]{1,0:T(8,128)S(1)}, f32[8,512]{1,0:T(8,128)}, u32[]{:S(2)}) copy-start(f32[8,512]{1,0:T(8,128)} %pad.42.refs_7_) | copy-start | bytes 49156
  103.8 21.9 %copy-start.42 = (f32[8,512]{1,0:T(8,128)S(1)}, f32[8,512]{1,0:T(8,128)}, u32[]{:S(2)}) copy-start(f32[8,512]{1,0:T(8,128)} %pad.43.refs_8_) | copy-start | bytes 49156
  103.8 55.4 %collective-permute-start.5 = (bf16[256,2048]{1,0:T(8,128)(2,1)}, bf16[256,2048]{1,0:T(8,128)(2,1)}, u32[]{:S(2)}, u32[]{:S(2)}) collective-permute-start(bf16[256,2048]{1,0:T(8,128)(2,1)} %broadcast_select_fusion), channel_id=1, source_target_pairs={{0,1},{1,0},{2,3},{3,2},{4,5},{5,4},{6,7},{7,6},{8,9},{9,8},{10,11... | collective-permute-start | bytes 3145736 | tf_op jit(solution)/shard_map/ppermute | solution.py:168
  124.7 34.4 %collective-permute-start.2 = (bf16[256,2048]{1,0:T(8,128)(2,1)}, bf16[256,2048]{1,0:T(8,128)(2,1)}, u32[]{:S(2)}, u32[]{:S(2)}) collective-permute-start(bf16[256,2048]{1,0:T(8,128)(2,1)} %broadcast_select_fusion.1), channel_id=1, source_target_pairs={{0,1},{1,0},{2,3},{3,2},{4,5},{5,4},{6,7},{7,6},{8,9},{9,8},{10,11... | collective-permute-start | bytes 3145736 | tf_op jit(solution)/shard_map/ppermute | solution.py:168
  135.9 1.8 copy-start.27
  136.6 20.9 %collective-permute-start.12 = (bf16[528,128]{1,0:T(8,128)(2,1)}, bf16[528,128]{1,0:T(8,128)(2,1)}, u32[]{:S(2)}, u32[]{:S(2)}) collective-permute-start(bf16[528,128]{1,0:T(8,128)(2,1)} %pad_maximum_fusion.1), channel_id=1, source_target_pairs={{0,2},{1,3},{2,0},{3,1},{4,6},{5,7},{6,4},{7,5},{8,10},{9,11},{10,... | collective-permute-start | bytes 405512 | tf_op jit(solution)/shard_map/ppermute | solution.py:168
  153.5 5.7 %copy-start.18 = (f32[512,128]{1,0:T(8,128)}, f32[512,128]{1,0:T(8,128)S(1)}, u32[]{:S(2)}) copy-start(f32[512,128]{1,0:T(8,128)S(1)} %get-tuple-element.43.refs_10_) | copy-start | bytes 786436
  154.2 22.6 %collective-permute-start.13 = (bf16[528,128]{1,0:T(8,128)(2,1)}, bf16[528,128]{1,0:T(8,128)(2,1)}, u32[]{:S(2)}, u32[]{:S(2)}) collective-permute-start(bf16[528,128]{1,0:T(8,128)(2,1)} %pad_maximum_fusion.2), channel_id=1, source_target_pairs={{0,14},{1,15},{2,4},{3,5},{4,2},{5,3},{6,8},{7,9},{8,6},{9,7},{10,... | collective-permute-start | bytes 405512 | tf_op jit(solution)/shard_map/ppermute | solution.py:168
  174.1 9.5 %copy-start.32 = (f32[512,128]{1,0:T(8,128)S(1)}, f32[512,128]{1,0:T(8,128)}, u32[]{:S(2)}) copy-start(f32[512,128]{1,0:T(8,128)} %copy-done.31) | copy-start | bytes 786436
  174.1 10.5 %copy-start.13 = (bf16[4,128,128]{2,1,0:T(8,128)(2,1)S(1)}, bf16[4,128,128]{2,1,0:T(8,128)(2,1)}, u32[]{:S(2)}) copy-start(bf16[4,128,128]{2,1,0:T(8,128)(2,1)} %vw_ref.3) | copy-start | bytes 393220
  174.2 10.5 %copy-start.34 = (bf16[128,128]{1,0:T(8,128)(2,1)S(1)}, bf16[128,128]{1,0:T(8,128)(2,1)}, u32[]{:S(2)}) copy-start(bf16[128,128]{1,0:T(8,128)(2,1)} %qw_ref.3) | copy-start | bytes 98308
  174.2 10.5 %copy-start.36 = (bf16[128,128]{1,0:T(8,128)(2,1)S(1)}, bf16[128,128]{1,0:T(8,128)(2,1)}, u32[]{:S(2)}) copy-start(bf16[128,128]{1,0:T(8,128)(2,1)} %kw_ref.3) | copy-start | bytes 98308
  174.2 7.2 %collective-permute-start.14 = (bf16[528,128]{1,0:T(8,128)(2,1)S(1)}, bf16[528,128]{1,0:T(8,128)(2,1)S(1)}, u32[]{:S(2)}, u32[]{:S(2)}) collective-permute-start(bf16[528,128]{1,0:T(8,128)(2,1)S(1)} %pad_maximum_fusion.3), channel_id=1, source_target_pairs={{0,15},{1,2},{2,1},{3,4},{4,3},{5,6},{6,5},{7,8},{8,7},{9,10},{10,... | collective-permute-start | bytes 405512 | tf_op jit(solution)/shard_map/ppermute | solution.py:168
  184.7 2.2 %copy-start.1 = (f32[512,2048]{1,0:T(8,128)S(1)}, f32[512,2048]{1,0:T(8,128)}, u32[]{:S(2)}) copy-start(f32[512,2048]{1,0:T(8,128)} %get-tuple-element.45.u_ref) | copy-start | bytes 12582916
  (33 other events, 27.4 us)
where the time goes:
time: 191 us; the launch traced here: 189 us
  local copies, waits for them, and re-layouts  70.2 us (37%)
  Pallas kernels  45.5 us (24%)
  other arithmetic  29.9 us (16%)
  waiting for transfers between devices  26 us (14%)
  starting transfers between devices  16.4 us (9%)
    pallas_call x5, Pallas kernels, run_block(): pl.pallas_call(functools.partial(block_kernel, len(cots), own, first, sca...  42.7 us
    unnamed x109, local copies, waits for them, and re-layouts  36.1 us
    ppermute x15, waiting for transfers between devices, send(): lax.ppermute(block, 'dom', [(i, rule(i) % domains) for i in range(domains)])  26 us
    ppermute x15, starting transfers between devices, send(): lax.ppermute(block, 'dom', [(i, rule(i) % domains) for i in range(domains)])  16.4 us
    slice x4, local copies, waits for them, and re-layouts, unpack(): qry = pack[:atoms]  6.27 us
    concatenate x1, local copies, waits for them, and re-layouts, shards(): jnp.concatenate([queries, positions.reshape(3 * atoms // 128, 128), jnp.z...  3.83 us
  transfers between devices with their start and end apart: 15, of which 3 were waited for; matrix products, arithmetic and copies ran while one was open for 31% of the time, Pallas kernels for 23%

commit v1 on v0

v1 whole, which is shorter than its diff:
```python
import functools

import jax
import jax.numpy as jnp
from jax import lax
from jax.experimental import pallas as pl
from jax.experimental.pallas import tpu as pltpu
from jax.sharding import PartitionSpec as P

TILE = 128
CUTOFF_SQ = 9.0
CHUNKS = 4
VMEM_BYTES = 48 * 2**20
F32 = jnp.float32
BF16 = jnp.bfloat16


def dot_nt(left, right):
    return lax.dot_general(left, right, (((1,), (1,)), ((), ())), preferred_element_type=F32)


def dot_tn(left, right):
    return lax.dot_general(left, right, (((0,), (0,)), ((), ())), preferred_element_type=F32)


def dot_nn(left, right):
    return lax.dot_general(left, right, (((1,), (0,)), ((), ())), preferred_element_type=F32)


def whole(n):
    return [pl.BlockSpec(memory_space=pltpu.VMEM)] * n


def block_terms(tables, acc, tgt, src, own, fwd, step, scale, cot_ref, qry_ref, meta_ref, slot):
    val_ref, key_ref, turn_ref = tables
    u_acc, k_acc, p_acc, q_src, p_src = acc
    cot = cot_ref[src, :]
    qry = qry_ref[src, :]
    grad = dot_nt(val_ref[tgt, :], cot)
    score = scale * dot_nt(key_ref[tgt, :], qry)
    keys = key_ref[tgt, :]
    turn = turn_ref[tgt, :]
    meta = meta_ref[:, src].astype(F32)
    if own:
        shift = 0.0
        keep = turn[:, 11:12] * meta[11:12]
        for b in range(1, 4):
            keep += turn[:, 11 + b : 12 + b] * meta[11 + b : 12 + b]
        row_id = lax.broadcasted_iota(jnp.int32, keep.shape, 0) + tgt.start
        col_id = lax.broadcasted_iota(jnp.int32, keep.shape, 1) + src.start
        keep = jnp.where(row_id == col_id, 0.0, keep)
    else:
        shift = jnp.where(fwd, float(step), -float(step))
        lent, used = 1 + 2 * step, 5 + 2 * step
        keep = None
        for b in range(2):
            row = jnp.where(fwd, turn[:, used + b : used + b + 1], turn[:, lent + b : lent + b + 1])
            col = jnp.where(fwd, meta[lent + b : lent + b + 1], meta[used + b : used + b + 1])
            keep = row * col if keep is None else keep + row * col
    diffs = [turn[:, x : x + 1] - (meta[x : x + 1] + (shift if x == 0 else 0.0)) for x in range(3)]
    dist = diffs[0] * diffs[0] + diffs[1] * diffs[1] + diffs[2] * diffs[2]
    inside = jnp.maximum(1.0 - dist * (1.0 / CUTOFF_SQ), 0.0)
    gate = jax.nn.sigmoid(score)
    half = keep * inside * gate
    weight = half * inside
    zgrad = (grad * weight * (1.0 - gate)).astype(BF16)
    push = (-4.0 / CUTOFF_SQ) * grad * half
    u_acc[tgt, :] += dot_nn(weight.astype(BF16), cot)
    k_acc[tgt, :] += scale * dot_nn(zgrad, qry)
    q_src[slot, src, :] += scale * dot_tn(zgrad, keys)
    for x in range(3):
        term = push * diffs[x]
        p_acc[tgt, x : x + 1] += jnp.sum(term, axis=1, keepdims=True)
        p_src[slot, x : x + 1, src] -= jnp.sum(term, axis=0, keepdims=True)


def layer_kernel(
    domains, scale,
    feat_ref, cot_ref, meta_ref, turn_ref, vw_ref, qw_ref, kw_ref,
    out_ref, force_ref,
    val_ref, qry_ref, key_ref, cots, qrys, metas,
    u_acc, k_acc, p_acc, q_src, p_src, q_out, p_out, q_back, p_back,
    send_sem, recv_sem,
):
    atoms = feat_ref.shape[0]
    chan = vw_ref.shape[1]
    rows = atoms // CHUNKS
    me = lax.axis_index("dom")
    core = lax.rem(me, 2)
    side = lax.rem(me // 2, 2)
    wrap = lambda i: lax.rem(i + domains, domains)
    twin = me + 1 - 2 * core
    across = me + 2 - 4 * side
    along = wrap(me + 4 - 8 * side)
    behind = wrap(me - 4 + 8 * side)
    far = wrap(me - 2 + 4 * side)
    near = wrap(me - 1 + 2 * core)
    straight = side == core

    barrier = pltpu.get_barrier_semaphore()
    for peer in (twin, across, along, behind, far, near):
        pl.semaphore_signal(
            barrier, inc=1, device_id={"dom": peer}, device_id_type=pl.DeviceIdType.MESH
        )

    def copy(src, dst, index, peer):
        return pltpu.make_async_remote_copy(
            src_ref=src,
            dst_ref=dst,
            send_sem=send_sem.at[index],
            recv_sem=recv_sem.at[index],
            device_id={"dom": peer},
            device_id_type=pl.DeviceIdType.MESH,
        )

    small = lambda q, m, slot, peer: (
        copy(q, qrys.at[slot], 2 * slot, peer),
        copy(m, metas.at[slot], 2 * slot + 1, peer),
    )
    piece = lambda ref, c: ref.at[c * rows : (c + 1) * rows]
    part = lambda slot, c: cots.at[slot, c * rows : (c + 1) * rows]
    big = lambda src, slot, c, peer: copy(piece(src, c), part(slot, c), 8 + slot * CHUNKS + c, peer)

    scalars = feat_ref[:, :chan]
    qry_ref[...] = dot_nn(scalars, qw_ref[...]).astype(BF16)
    pl.semaphore_wait(barrier, 6)
    sent = []

    def begin(copies):
        for item in copies:
            item.start()
            sent.append(item)

    small_1 = small(qry_ref, meta_ref, 1, across)
    small_0 = small(qry_ref, meta_ref, 0, twin)
    begin(small_1)
    big_1 = [big(cot_ref, 1, c, across) for c in range(CHUNKS)]
    begin(big_1)
    begin(small_0)
    big_0 = [big(cot_ref, 0, c, twin) for c in range(CHUNKS)]
    begin(big_0)

    key_ref[...] = dot_nn(scalars, kw_ref[...]).astype(BF16)
    for comp in range(16):
        cols = slice(comp * chan, (comp + 1) * chan)
        val_ref[:, cols] = dot_nn(feat_ref[:, cols], vw_ref[int(comp**0.5)]).astype(BF16)
    for ref in (u_acc, k_acc, p_acc, q_src, p_src):
        ref[...] = jnp.zeros_like(ref)
    p_out[...] = jnp.zeros_like(p_out)

    small_2 = small(qrys.at[1], metas.at[1], 2, along)
    small_3a = small(qrys.at[1], metas.at[1], 3, twin)
    small_3b = small(qrys.at[2], metas.at[2], 3, twin)
    big_2 = [big(cots.at[1], 2, c, along) for c in range(CHUNKS)]
    big_3a = [big(cots.at[1], 3, c, twin) for c in range(CHUNKS)]
    big_3b = [big(cots.at[2], 3, c, twin) for c in range(CHUNKS)]

    def when_start(flag, copies):
        @pl.when(flag)
        def _():
            for item in copies:
                item.start()

    crooked = jnp.logical_not(straight)
    tables = (val_ref, key_ref, turn_ref)
    acc = (u_acc, k_acc, p_acc, q_src, p_src)
    height = 2 * TILE

    def block(first, width, own, fwd, step, cot, qry, meta, slot):
        def visit(r, carry):
            tgt = pl.ds(pl.multiple_of(r * height, height), height)
            block_terms(tables, acc, tgt, pl.ds(first, width), own, fwd, step, scale, cot, qry, meta, slot)
            return carry

        lax.fori_loop(0, atoms // height, visit, 0)

    forward = [core == 0, side == 0, side == 1, core == 1]
    steps = [1, 2, 2, 1]

    def remote(slot, first, width):
        block(
            first, width, False, forward[slot], steps[slot],
            cots.at[slot], qrys.at[slot], metas.at[slot], slot,
        )

    backs = []

    def give_back(slot, peer):
        q_out[slot] = q_src[slot].astype(BF16)
        p_out[slot, 0:8] = p_src[slot].astype(BF16)
        base = 8 + 4 * CHUNKS + 2 * slot
        pair = (
            copy(q_out.at[slot], q_back.at[slot], base, peer),
            copy(p_out.at[slot], p_back.at[slot], base + 1, peer),
        )
        begin(pair)
        backs.extend(pair)

    def arrived(copies):
        for item in copies:
            item.wait_recv()

    for first in range(0, atoms, height):
        block(first, height, True, None, 0, cot_ref, qry_ref, meta_ref, 4)
    arrived(small_1)
    begin(small_2)
    when_start(straight, small_3a)
    arrived(small_0)
    arrived(big_0)
    remote(0, 0, height)
    arrived(small_2)
    when_start(crooked, small_3b)
    for c in range(CHUNKS + 2):
        if c < CHUNKS:
            arrived([big_1[c]])
            begin([big_2[c]])
            when_start(straight, [big_3a[c]])
        if c == 0:
            for first in range(height, atoms, height):
                remote(0, first, height)
            give_back(0, twin)
        if c < CHUNKS:
            remote(1, c * rows, rows)
            if c == CHUNKS - 1:
                give_back(1, across)
        if 1 <= c <= CHUNKS:
            arrived([big_2[c - 1]])
            when_start(crooked, [big_3b[c - 1]])
            remote(2, (c - 1) * rows, rows)
            if c == CHUNKS:
                give_back(2, far)
        if c >= 2:
            if c == 2:
                arrived(small_3a)
            arrived([big_3a[c - 2]])
            remote(3, (c - 2) * rows, rows)
    give_back(3, near)
    for comp in range(1, 16):
        cols = slice(comp * chan, (comp + 1) * chan)
        out_ref[:, cols] = dot_nt(u_acc[:, cols].astype(BF16), vw_ref[int(comp**0.5)]).astype(BF16)
    total_p = p_acc[...].T[0:8] + p_src[4]
    total_q = q_src[4]
    arrived(backs)
    for slot in range(4):
        total_q = total_q + q_back[slot].astype(F32)
        total_p = total_p + p_back[slot].astype(F32)[0:8]
    mixed = dot_nt(u_acc[:, :chan].astype(BF16), vw_ref[0])
    mixed += dot_nt(total_q.astype(BF16), qw_ref[...])
    mixed += dot_nt(k_acc[...].astype(BF16), kw_ref[...])
    out_ref[:, :chan] = mixed.astype(BF16)
    force_ref[...] = -total_p[0:3]
    for item in sent:
        item.wait_send()
    for item in (*small_3a, *big_3a):
        item.wait_send()


def shards(
    features, cotangent, positions, value_weight, query_weight, key_weight, ghost_index, tile_pairs, tile_counts
):
    atoms, feat = features.shape
    width = query_weight.shape[1]
    slots = tile_pairs.shape[2]
    tiles = atoms // TILE
    gtiles = ghost_index.shape[2] // TILE
    domains = lax.axis_size("dom")

    used = jnp.arange(slots, dtype=jnp.int32)[None, :] < tile_counts[0][:, None]
    ids = jnp.arange(tiles, dtype=jnp.int32)
    hit_a = tile_pairs[0, :, :, 0, None] == ids
    hit_b = tile_pairs[0, :, :, 1, None] == ids
    active = jnp.sum(
        (hit_a[:, :, :, None] & hit_b[:, :, None, :] & used[:, :, None, None]).astype(F32), axis=1
    )
    intra = jnp.maximum(active[0], active[0].T)
    atom_ids = jnp.arange(atoms, dtype=jnp.int32)
    listed = ghost_index[0].reshape(2 * gtiles, TILE)
    ghost_rows = jnp.sum((listed[:, :, None] == atom_ids).astype(F32), axis=1)
    act_tiles = active[1:, :, :gtiles].transpose(0, 2, 1).reshape(2 * gtiles, tiles)
    one_hot = jnp.eye(tiles, dtype=F32)
    spread = lambda table: jnp.repeat(table, TILE, axis=1)
    blank = jnp.zeros((1, atoms), F32)
    points = positions.astype(F32)
    shared = [points, ghost_rows, spread(act_tiles)]
    meta = jnp.concatenate([*shared, spread(one_hot), blank], axis=0).astype(BF16)
    turn = jnp.concatenate([*shared, spread(intra), blank], axis=0).T
    vmem = pltpu.VMEM
    adjoint, forces = pl.pallas_call(
        functools.partial(layer_kernel, domains, width ** (-0.5)),
        out_shape=[
            jax.ShapeDtypeStruct((atoms, feat), BF16),
            jax.ShapeDtypeStruct((3, atoms), F32),
        ],
        in_specs=whole(7),
        out_specs=whole(2),
        scratch_shapes=[
            vmem((atoms, feat), BF16),
            vmem((atoms, width), BF16),
            vmem((atoms, width), BF16),
            vmem((4, atoms, feat), BF16),
            vmem((4, atoms, width), BF16),
            vmem((4, 16, atoms), BF16),
            vmem((atoms, feat), F32),
            vmem((atoms, width), F32),
            vmem((atoms, 128), F32),
            vmem((5, atoms, width), F32),
            vmem((5, 8, atoms), F32),
            vmem((4, atoms, width), BF16),
            vmem((4, 16, atoms), BF16),
            vmem((4, atoms, width), BF16),
            vmem((4, 16, atoms), BF16),
            pltpu.SemaphoreType.DMA((16 + 4 * CHUNKS,)),
            pltpu.SemaphoreType.DMA((16 + 4 * CHUNKS,)),
        ],
        compiler_params=pltpu.CompilerParams(
            vmem_limit_bytes=VMEM_BYTES, collective_id=0, has_side_effects=True
        ),
    )(features, cotangent, meta, turn, value_weight, query_weight, key_weight)
    return adjoint, forces


def solution(mesh):
    both = ("groups", "dom")
    placed = (
        P(both, None),
        P(both, None),
        P(None, both),
        P(),
        P(),
        P(),
        P(both, None, None),
        P(both, None, None, None),
        P(both, None),
    )
    return jax.shard_map(
        shards, mesh=mesh, in_specs=placed, out_specs=(P(both, None), P(None, both)), check_vma=False
    )
```

time: 191 us -> 93 us (0.49)
  local copies, waits for them, and re-layouts: 70.2 us -> 9.6 us
  Pallas kernels: 45.5 us -> 80.6 us
  other arithmetic: 29.9 us -> 1.05 us
  waiting for transfers between devices: 26 us -> 0 us
  starting transfers between devices: 16.4 us -> 0 us
    pallas_call x7 -> x1, Pallas kernels: 45.5 us -> 80.6 us  [shards(): pl.pallas_call(functools.partial(layer_kernel, domains, width ** (-0.5)),...]
    unnamed x109 -> x18, local copies, waits for them, and re-layouts: 36.1 us -> 6.17 us
    ppermute x15 -> x0, waiting for transfers between devices: 26 us -> none  [send(): lax.ppermute(block, 'dom', [(i, rule(i) % domains) for i in range(domains)])]
    ppermute x15 -> x0, starting transfers between devices: 16.4 us -> none  [send(): lax.ppermute(block, 'dom', [(i, rule(i) % domains) for i in range(domains)])]
    slice x24 -> x0, local copies, waits for them, and re-layouts: 15.5 us -> none  [the longest x4 6.27 us: unpack(): qry = pack[:atoms]]
    select_n x9 -> x0, other arithmetic: 11.3 us -> none  [the longest x2 3.58 us: unpack(): row = jnp.where(forward, act_rows[step - 1], ghost_rows[step - 1])]
    pad x11 -> x0, local copies, waits for them, and re-layouts: 7.19 us -> none  [the longest x4 3.09 us: unpack(): return ((qry, ps, jnp.pad(col, ((0, 8 - gtiles), (0, 0)))), row.T)]
    add x5 -> x0, other arithmetic: 4.1 us -> none  [the longest x4 3 us: unpack(): pos + jnp.array([1.0, 0.0, 0.0], F32)[:, None] * shift]
  transfers between devices with their start and end apart: 15 -> 0, of which waited for: 3 -> 0; matrix products, arithmetic and copies ran while one was open for 31% -> 0% of each run, Pallas kernels for 23% -> 0%
where the time goes in v1:
time: 93 us; the launch traced here: 91.9 us
  Pallas kernels  80.6 us (87%)
  local copies, waits for them, and re-layouts  9.6 us (10%)
  other arithmetic  1.05 us (1%)
    pallas_call x1, Pallas kernels, shards(): pl.pallas_call(functools.partial(layer_kernel, domains, width ** (-0.5)),...  80.6 us
    unnamed x18, local copies, waits for them, and re-layouts  6.17 us

profile of v1, /device:TPU:0, one launch (start us, length us, event | category | flops | bytes accessed | tf_op | source)
XLA Modules:
  0.0 91.9 jit_solution(10848981703175062669)
XLA Ops:
  0.6 0.7 iota_compare_fusion.4
  1.4 0.7 eq.56
  2.1 0.1 broadcast_bitcast_fusion.2
  2.1 0.8 fusion.1
  2.9 0.1 convert_reduce_fusion.1
  3.0 0.1 copy.29
  3.1 0.1 copy.28
  3.2 0.1 broadcast_bitcast_fusion.1
  3.3 0.2 convert_reduce_fusion
  3.5 0.8 concatenate.7.meta_ref
  4.4 0.1 broadcast_bitcast_fusion
  4.4 0.8 concatenate.8
  5.3 0.1 copy.30
  5.4 0.0 copy-start
  5.4 1.6 %copy-done = bf16[512,2048]{1,0:T(8,128)(2,1)S(1)} copy-done((bf16[512,2048]{1,0:T(8,128)(2,1)S(1)}, bf16[512,2048]{1,0:T(8,128)(2,1)}, u32[]{:S(2)}) %copy-start) | copy-done | bytes 2097176
  7.0 0.0 copy-start.1
  7.0 0.9 copy-done.1
  7.9 0.0 copy-start.2
  7.9 0.8 copy-done.2
  8.7 0.0 copy-start.3
  8.7 0.8 copy-done.3
  9.4 80.6 %shard_map.104 = (bf16[512,2048]{1,0:T(8,128)(2,1)S(1)}, f32[3,512]{1,0:T(4,128)S(1)}) custom-call(bf16[512,2048]{1,0:T(8,128)(2,1)S(1)} %copy-done, bf16[512,2048]{1,0:T(8,128)(2,1)} %cot_ref.1, bf16[16,512]{1,0:T(8,128)(2,1)S(1)} %concatenate.7.meta_ref, f32[512,16]{1,0:T(8,128)S(1)} %bitcast.33, bf16[4,128,128]{2,1,0:T(8,128)(2,1)S(1)} %copy-done.1, ...), custom_call_target="tpu_custom_call" | custom-call | tf_op jit(solution)/shard_map/pallas_call | solution.py:288
  90.0 1.3 %copy.49 = bf16[512,2048]{1,0:T(8,128)(2,1)} copy(bf16[512,2048]{1,0:T(8,128)(2,1)S(1)} %get-tuple-element.8) | data formatting | bytes 4194304
  91.3 0.6 copy.50
  (14 shorter events, 0.1 us)
Async XLA Ops:
  5.4 1.6 %copy-start = (bf16[512,2048]{1,0:T(8,128)(2,1)S(1)}, bf16[512,2048]{1,0:T(8,128)(2,1)}, u32[]{:S(2)}) copy-start(bf16[512,2048]{1,0:T(8,128)(2,1)} %feat_ref.1) | copy-start | bytes 6291460
  7.0 0.9 copy-start.1
  7.9 0.8 copy-start.2
  8.7 0.8 copy-start.3
